TPU v7x, 32 devices: a whole 2x2x4 slice. The times are simulated.
32 devices in a mesh: row: 8 (over z, core), col: 4 (over y, x).
Axes of the slice: x: 2, y: 2, z: 4, core: 2. Of those that a mesh axis runs over, the one named last changes fastest.
Arguments:
- a_blocks: bfloat16 [8, 4, 32, 128, 128], P('row', 'col'), may hold values from -6 to 6
- a_coord: int32 [8, 4, 32, 2], P('row', 'col'), may hold values from -1 to 31, as said below
- b_blocks: bfloat16 [8, 4, 32, 128, 128], P('row', 'col'), may hold values from -0.125 to 0.125
- b_coord: int32 [8, 4, 32, 2], P('row', 'col'), may hold values from -1 to 31, as said below
- c_mask: int32 [32, 32], P('row', 'col'), may hold values 0 or 1
Outputs:
- c_blocks: float32 [4096, 4096], P('row', 'col')
Inputs may be any that keep to these rules, and one draw needn't show every extreme that they name: `a_coord`: entry [i, s, t] holds the block row and block column of the block in slot t of device (i, s), or -1 in both for an empty slot. Its block row lies in i * 4 to (i + 1) * 4 - 1. With p = column // 4, slot t lies in t // 8 = (p - i) mod 4. No block is named twice. `b_coord`: entry [s, j, t] holds the block row and block column of the block in slot t of device (s, j), or -1 in both for an empty slot. Its block column lies in j * 8 to (j + 1) * 8 - 1. With p = row // 4, slot t lies in t // 4 = (p - j) mod 8. No block is named twice.
All inputs are finite; a program needn't handle non-finite values. No bound on the sum of `c_mask` on one device may be relied on, other than what follows from the above.
Results may differ from a plain program's by a relative error of at most 0.0003.
Values may be sent and summed in bfloat16 or wider, within the bound.
A program may use at most 64 MiB of HBM per device.

v0:
```python
import jax
import jax.numpy as jnp
from jax import lax
from jax.sharding import PartitionSpec as P


def passed_along(value, axis, steps):
    count = lax.axis_size(axis)
    pairs = [(source, (source + steps) % count) for source in range(count)]
    return lax.ppermute(value, axis, pairs)


def roll_panel(panel_b):
    return passed_along(panel_b, "row", -1)


def shards(a_blocks, a_coord, b_blocks, b_coord, c_mask):
    row_count = lax.axis_size("row")
    col_count = lax.axis_size("col")
    panel_ratio = row_count // col_count
    grid_row = lax.axis_index("row")
    grid_col = lax.axis_index("col")
    block_size = a_blocks.shape[-1]
    band_rows = c_mask.shape[0]
    band_cols = c_mask.shape[1]
    a_send = a_blocks.reshape(col_count, -1, block_size, block_size)
    a_tags = a_coord.reshape(col_count, -1, 2)
    a_recv, a_tags = (
        lax.all_to_all(a_send, "col", split_axis=0, concat_axis=0, tiled=True),
        lax.all_to_all(a_tags, "col", split_axis=0, concat_axis=0, tiled=True),
    )
    a_recv = a_recv.reshape(-1, block_size, block_size)
    a_tags = a_tags.reshape(-1, 2)
    a_live = a_tags[:, 0] >= 0
    panel_index = a_tags[:, 1] // band_rows
    count_a = panel_ratio * band_rows * band_rows
    a_pos = (
        panel_index // col_count * band_rows * band_rows
        + (a_tags[:, 0] - grid_row * band_rows) * band_rows
        + a_tags[:, 1] % band_rows
    )
    a_pos = jnp.where(a_live, a_pos, count_a)
    a_tile = (
        jnp.zeros((count_a, block_size, block_size), a_blocks.dtype)
        .at[a_pos]
        .set(a_recv, mode="drop")
    )
    a_group = a_tile.reshape(panel_ratio, band_rows, band_rows, block_size, block_size)
    a_group = a_group.transpose(0, 1, 3, 2, 4).reshape(
        panel_ratio, band_rows * block_size, band_rows * block_size
    )
    b_send = b_blocks.reshape(row_count, -1, block_size, block_size)
    b_tags = b_coord.reshape(row_count, -1, 2)
    b_recv, b_tags = (
        lax.all_to_all(b_send, "row", split_axis=0, concat_axis=0, tiled=True),
        lax.all_to_all(b_tags, "row", split_axis=0, concat_axis=0, tiled=True),
    )
    b_recv = b_recv.reshape(-1, block_size, block_size)
    b_tags = b_tags.reshape(-1, 2)
    b_live = b_tags[:, 0] >= 0
    count_b = band_rows * band_cols
    b_pos = b_tags[:, 0] % band_rows * band_cols + b_tags[:, 1] - grid_col * band_cols
    b_pos = jnp.where(b_live, b_pos, count_b)
    b_tile = (
        jnp.zeros((count_b, block_size, block_size), b_blocks.dtype)
        .at[b_pos]
        .set(b_recv, mode="drop")
    )
    b_panel = b_tile.reshape(band_rows, band_cols, block_size, block_size)
    b_panel = b_panel.transpose(0, 2, 1, 3).reshape(band_rows * block_size, band_cols * block_size)
    offset = grid_row + grid_col
    accumulated = jnp.zeros((band_rows * block_size, band_cols * block_size), jnp.float32)

    def advance(step_index, carried):
        a_current, panel_b, running = carried
        member = (offset + step_index) % row_count // col_count
        a_use = lax.dynamic_index_in_dim(a_current, member, 0, keepdims=False)
        running = running + jnp.dot(a_use, panel_b, preferred_element_type=jnp.float32)
        a_current = passed_along(a_current, "col", -1)
        return (a_current, roll_panel(panel_b), running)

    a_last, b_last, accumulated = lax.fori_loop(
        0, row_count - 1, advance, (a_group, b_panel, accumulated)
    )
    member = (offset + row_count - 1) % row_count // col_count
    a_use = lax.dynamic_index_in_dim(a_last, member, 0, keepdims=False)
    accumulated = accumulated + jnp.dot(a_use, b_last, preferred_element_type=jnp.float32)
    masked = accumulated.reshape(band_rows, block_size, band_cols, block_size) * c_mask[
        :, None, :, None
    ].astype(jnp.float32)
    return masked.reshape(band_rows * block_size, band_cols * block_size)


def solution(mesh):
    placed = (
        P("row", "col", None, None, None),
        P("row", "col", None, None),
        P("row", "col", None, None, None),
        P("row", "col", None, None),
        P("row", "col"),
    )
    return jax.shard_map(
        shards, mesh=mesh, in_specs=placed, out_specs=P("row", "col"), check_vma=False
    )
```

profile of v0, /device:TPU:0, one launch (start us, length us, event | category | flops | bytes accessed | tf_op | source)
XLA Modules:
  0.0 258.3 jit_solution(16308488505931294219)
XLA Ops:
  1.4 5.2 %all-to-all-start = ((s32[4,8,2]{1,2,0:T(2,128)}), s32[4,8,2]{1,2,0:T(2,128)S(1)}, u32[]{:S(2)}, u32[]{:S(2)}) async-start(s32[4,8,2]{1,2,0:T(2,128)} %copy.8), calls=%async_computation | async-start | bytes 8192 | tf_op jit(solution)/shard_map/all_to_all | solution.py:30
  7.3 3.9 %all-to-all-done = s32[4,8,2]{1,2,0:T(2,128)S(1)} async-done(((s32[4,8,2]{1,2,0:T(2,128)}), s32[4,8,2]{1,2,0:T(2,128)S(1)}, u32[]{:S(2)}, u32[]{:S(2)}) %all-to-all-start) | async-done | bytes 288 | tf_op jit(solution)/shard_map/all_to_all | solution.py:30
  11.2 10.3 %all_to_all.20 = s32[8,4,2]{1,2,0:T(2,128)S(1)} all-to-all(s32[8,4,2]{1,2,0:T(2,128)S(1)} %copy.11), channel_id=1, replica_groups=mesh['row'=8,'col'=4] {'row'}, dimensions={0} | all-to-all | bytes 512 | tf_op jit(solution)/shard_map/all_to_all | solution.py:56
  21.5 18.8 %all_to_all.21 = bf16[4,8,128,128]{3,2,1,0:T(8,128)(2,1)} all-to-all(bf16[4,8,128,128]{3,2,1,0:T(8,128)(2,1)} %bitcast.48), channel_id=1, replica_groups=mesh['row'=8,'col'=4] {'col'}, dimensions={0} | all-to-all | bytes 2097152 | tf_op jit(solution)/shard_map/all_to_all | solution.py:29
  40.3 4.2 %all-to-all-start.3 = ((bf16[8,4,128,128]{3,2,1,0:T(8,128)(2,1)}), bf16[8,4,128,128]{3,2,1,0:T(8,128)(2,1)}, u32[]{:S(2)}, u32[]{:S(2)}) async-start(bf16[8,4,128,128]{3,2,1,0:T(8,128)(2,1)} %bitcast.6), calls=%async_computation.3 | async-start | bytes 2097152 | tf_op jit(solution)/shard_map/all_to_all | solution.py:55
  45.1 3.6 %scatter_fusion = bf16[32,128,128]{2,1,0:T(8,128)(2,1)S(1)} fusion(bf16[32,128,128]{2,1,0:T(8,128)(2,1)S(1)} %broadcast.69.clone, s32[32]{0:T(128)S(1)} %fusion.9, bf16[32,128,128]{2,1,0:T(8,128)(2,1)} %bitcast.46), kind=kCustom, calls=%fused_computation | custom fusion | bytes 3145856 | tf_op jit(solution)/shard_map/scatter | solution.py:46
  52.7 18.4 %all-to-all-done.3 = bf16[8,4,128,128]{3,2,1,0:T(8,128)(2,1)} async-done(((bf16[8,4,128,128]{3,2,1,0:T(8,128)(2,1)}), bf16[8,4,128,128]{3,2,1,0:T(8,128)(2,1)}, u32[]{:S(2)}, u32[]{:S(2)}) %all-to-all-start.3) | async-done | bytes 1048608 | tf_op jit(solution)/shard_map/all_to_all | solution.py:55
  71.4 3.6 %scatter_fusion.1 = bf16[32,128,128]{2,1,0:T(8,128)(2,1)S(1)} fusion(bf16[32,128,128]{2,1,0:T(8,128)(2,1)S(1)} %broadcast.69.clone.1, s32[32]{0:T(128)S(1)} %fusion.10, bf16[32,128,128]{2,1,0:T(8,128)(2,1)} %bitcast.7), kind=kCustom, calls=%fused_computation.1 | custom fusion | bytes 3145856 | tf_op jit(solution)/shard_map/scatter | solution.py:67
  76.9 177.6 %while.20 = (s32[]{:T(128)}, bf16[2,512,512]{2,1,0:T(8,128)(2,1)}, bf16[512,1024]{1,0:T(8,128)(2,1)}, f32[512,1024]{1,0:T(8,128)S(1)}, s32[]{:T(128)}, /*index=5...) while((s32[]{:T(128)}, bf16[2,512,512]{2,1,0:T(8,128)(2,1)}, ...), condition=%wide.region_3.4_spmd.clone, body=%wide.region_2.3_spmd.clone.sunk | while | flops 537919488 | bytes 18350596 | solution.py:82
  84.0 20.2 %collective-permute-done = bf16[2,512,512]{2,1,0:T(8,128)(2,1)} collective-permute-done((bf16[2,512,512]{2,1,0:T(8,128)(2,1)}, bf16[2,512,512]{2,1,0:T(8,128)(2,1)}, u32[]{:S(2)}, u32[]{:S(2)}) %collective-permute-start) | collective-permute-done | bytes 1048608 | tf_op jit(solution)/shard_map/while/body/eval_jaxpr/ppermute | solution.py:10
  104.2 2.3 copy.26
  111.8 18.9 %collective-permute-done = bf16[2,512,512]{2,1,0:T(8,128)(2,1)} collective-permute-done((bf16[2,512,512]{2,1,0:T(8,128)(2,1)}, bf16[2,512,512]{2,1,0:T(8,128)(2,1)}, u32[]{:S(2)}, u32[]{:S(2)}) %collective-permute-start) | collective-permute-done | bytes 1048608 | tf_op jit(solution)/shard_map/while/body/eval_jaxpr/ppermute | solution.py:10
  132.9 2.6 %collective-permute-start = (bf16[2,512,512]{2,1,0:T(8,128)(2,1)}, bf16[2,512,512]{2,1,0:T(8,128)(2,1)}, u32[]{:S(2)}, u32[]{:S(2)}) collective-permute-start(bf16[2,512,512]{2,1,0:T(8,128)(2,1)} %copy.26), channel_id=1, source_target_pairs={{0,3},{1,0},{2,1},{3,2},{4,7},{5,4},{6,5},{7,6},{8,11},{9,8},{10,9... | collective-permute-start | bytes 3145736 | tf_op jit(solution)/shard_map/while/body/eval_jaxpr/ppermute | solution.py:10
  138.9 18.2 %collective-permute-done = bf16[2,512,512]{2,1,0:T(8,128)(2,1)} collective-permute-done((bf16[2,512,512]{2,1,0:T(8,128)(2,1)}, bf16[2,512,512]{2,1,0:T(8,128)(2,1)}, u32[]{:S(2)}, u32[]{:S(2)}) %collective-permute-start) | collective-permute-done | bytes 1048608 | tf_op jit(solution)/shard_map/while/body/eval_jaxpr/ppermute | solution.py:10
  157.0 2.3 copy.26
  159.3 2.6 %collective-permute-start = (bf16[2,512,512]{2,1,0:T(8,128)(2,1)}, bf16[2,512,512]{2,1,0:T(8,128)(2,1)}, u32[]{:S(2)}, u32[]{:S(2)}) collective-permute-start(bf16[2,512,512]{2,1,0:T(8,128)(2,1)} %copy.26), channel_id=1, source_target_pairs={{0,3},{1,0},{2,1},{3,2},{4,7},{5,4},{6,5},{7,6},{8,11},{9,8},{10,9... | collective-permute-start | bytes 3145736 | tf_op jit(solution)/shard_map/while/body/eval_jaxpr/ppermute | solution.py:10
  165.2 17.2 %collective-permute-done = bf16[2,512,512]{2,1,0:T(8,128)(2,1)} collective-permute-done((bf16[2,512,512]{2,1,0:T(8,128)(2,1)}, bf16[2,512,512]{2,1,0:T(8,128)(2,1)}, u32[]{:S(2)}, u32[]{:S(2)}) %collective-permute-start) | collective-permute-done | bytes 1048608 | tf_op jit(solution)/shard_map/while/body/eval_jaxpr/ppermute | solution.py:10
  184.7 2.6 %collective-permute-start = (bf16[2,512,512]{2,1,0:T(8,128)(2,1)}, bf16[2,512,512]{2,1,0:T(8,128)(2,1)}, u32[]{:S(2)}, u32[]{:S(2)}) collective-permute-start(bf16[2,512,512]{2,1,0:T(8,128)(2,1)} %copy.26), channel_id=1, source_target_pairs={{0,3},{1,0},{2,1},{3,2},{4,7},{5,4},{6,5},{7,6},{8,11},{9,8},{10,9... | collective-permute-start | bytes 3145736 | tf_op jit(solution)/shard_map/while/body/eval_jaxpr/ppermute | solution.py:10
  190.7 16.3 %collective-permute-done = bf16[2,512,512]{2,1,0:T(8,128)(2,1)} collective-permute-done((bf16[2,512,512]{2,1,0:T(8,128)(2,1)}, bf16[2,512,512]{2,1,0:T(8,128)(2,1)}, u32[]{:S(2)}, u32[]{:S(2)}) %collective-permute-start) | collective-permute-done | bytes 1048608 | tf_op jit(solution)/shard_map/while/body/eval_jaxpr/ppermute | solution.py:10
  209.3 2.6 %collective-permute-start = (bf16[2,512,512]{2,1,0:T(8,128)(2,1)}, bf16[2,512,512]{2,1,0:T(8,128)(2,1)}, u32[]{:S(2)}, u32[]{:S(2)}) collective-permute-start(bf16[2,512,512]{2,1,0:T(8,128)(2,1)} %copy.26), channel_id=1, source_target_pairs={{0,3},{1,0},{2,1},{3,2},{4,7},{5,4},{6,5},{7,6},{8,11},{9,8},{10,9... | collective-permute-start | bytes 3145736 | tf_op jit(solution)/shard_map/while/body/eval_jaxpr/ppermute | solution.py:10
  215.2 15.4 %collective-permute-done = bf16[2,512,512]{2,1,0:T(8,128)(2,1)} collective-permute-done((bf16[2,512,512]{2,1,0:T(8,128)(2,1)}, bf16[2,512,512]{2,1,0:T(8,128)(2,1)}, u32[]{:S(2)}, u32[]{:S(2)}) %collective-permute-start) | collective-permute-done | bytes 1048608 | tf_op jit(solution)/shard_map/while/body/eval_jaxpr/ppermute | solution.py:10
  232.9 2.6 %collective-permute-start = (bf16[2,512,512]{2,1,0:T(8,128)(2,1)}, bf16[2,512,512]{2,1,0:T(8,128)(2,1)}, u32[]{:S(2)}, u32[]{:S(2)}) collective-permute-start(bf16[2,512,512]{2,1,0:T(8,128)(2,1)} %copy.26), channel_id=1, source_target_pairs={{0,3},{1,0},{2,1},{3,2},{4,7},{5,4},{6,5},{7,6},{8,11},{9,8},{10,9... | collective-permute-start | bytes 3145736 | tf_op jit(solution)/shard_map/while/body/eval_jaxpr/ppermute | solution.py:10
  238.8 15.7 %collective-permute-done = bf16[2,512,512]{2,1,0:T(8,128)(2,1)} collective-permute-done((bf16[2,512,512]{2,1,0:T(8,128)(2,1)}, bf16[2,512,512]{2,1,0:T(8,128)(2,1)}, u32[]{:S(2)}, u32[]{:S(2)}) %collective-permute-start) | collective-permute-done | bytes 1048608 | tf_op jit(solution)/shard_map/while/body/eval_jaxpr/ppermute | solution.py:10
  254.7 3.6 %bitcast_multiply_fusion = f32[512,1024]{1,0:T(8,128)} fusion(f32[64,8,8,128]{3,2,1,0:T(8,128)S(1)} %bitcast.45, f32[512,1024]{1,0:T(8,128)S(1)} %get-tuple-element.142, bf16[512,1024]{1,0:T(8,128)(2,1)} %get-tuple-element.144, bf16[2,512,512]{2,1,0:T(8,128)(2,1)} %get-tuple-element.143, s32[]{:T(128)S(6)} %select_n.101), kind=kOutput, calls=%fused_computation.6 | convolution fusion | flops 537919488 | bytes 7864324 | tf_op jit(solution)/shard_map/dot_general | solution.py:87
  (56 shorter events, 46.9 us)
Async XLA Ops:
  1.4 9.8 %all-to-all-start = ((s32[4,8,2]{1,2,0:T(2,128)}), s32[4,8,2]{1,2,0:T(2,128)S(1)}, u32[]{:S(2)}, u32[]{:S(2)}) async-start(s32[4,8,2]{1,2,0:T(2,128)} %copy.8), calls=%async_computation | async-start | bytes 8192 | tf_op jit(solution)/shard_map/all_to_all | solution.py:30
  21.5 23.1 %copy-start = (s32[4,8]{1,0:T(4,128)S(1)}, s32[4,8]{1,0:T(4,128)}, u32[]{:S(2)}) copy-start(s32[4,8]{1,0:T(4,128)} %param.11) | copy-start | bytes 388
  40.3 30.8 %all-to-all-start.3 = ((bf16[8,4,128,128]{3,2,1,0:T(8,128)(2,1)}), bf16[8,4,128,128]{3,2,1,0:T(8,128)(2,1)}, u32[]{:S(2)}, u32[]{:S(2)}) async-start(bf16[8,4,128,128]{3,2,1,0:T(8,128)(2,1)} %bitcast.6), calls=%async_computation.3 | async-start | bytes 2097152 | tf_op jit(solution)/shard_map/all_to_all | solution.py:55
  79.2 25.0 %collective-permute-start = (bf16[2,512,512]{2,1,0:T(8,128)(2,1)}, bf16[2,512,512]{2,1,0:T(8,128)(2,1)}, u32[]{:S(2)}, u32[]{:S(2)}) collective-permute-start(bf16[2,512,512]{2,1,0:T(8,128)(2,1)} %copy.26), channel_id=1, source_target_pairs={{0,3},{1,0},{2,1},{3,2},{4,7},{5,4},{6,5},{7,6},{8,11},{9,8},{10,9... | collective-permute-start | bytes 3145736 | tf_op jit(solution)/shard_map/while/body/eval_jaxpr/ppermute | solution.py:10
  81.3 22.9 %collective-permute-start.1 = (bf16[512,1024]{1,0:T(8,128)(2,1)S(1)}, bf16[512,1024]{1,0:T(8,128)(2,1)}, u32[]{:S(2)}, u32[]{:S(2)}) collective-permute-start(bf16[512,1024]{1,0:T(8,128)(2,1)S(1)} %copy.27), channel_id=1, source_target_pairs={{0,28},{4,0},{8,4},{12,8},{16,12},{20,16},{24,20},{28,24},{1,29},{... | collective-permute-start | bytes 3145736 | tf_op jit(solution)/shard_map/while/body/eval_jaxpr/ppermute | solution.py:10
  106.5 24.2 %collective-permute-start = (bf16[2,512,512]{2,1,0:T(8,128)(2,1)}, bf16[2,512,512]{2,1,0:T(8,128)(2,1)}, u32[]{:S(2)}, u32[]{:S(2)}) collective-permute-start(bf16[2,512,512]{2,1,0:T(8,128)(2,1)} %copy.26), channel_id=1, source_target_pairs={{0,3},{1,0},{2,1},{3,2},{4,7},{5,4},{6,5},{7,6},{8,11},{9,8},{10,9... | collective-permute-start | bytes 3145736 | tf_op jit(solution)/shard_map/while/body/eval_jaxpr/ppermute | solution.py:10
  109.5 21.2 %collective-permute-start.1 = (bf16[512,1024]{1,0:T(8,128)(2,1)S(1)}, bf16[512,1024]{1,0:T(8,128)(2,1)}, u32[]{:S(2)}, u32[]{:S(2)}) collective-permute-start(bf16[512,1024]{1,0:T(8,128)(2,1)S(1)} %copy.27), channel_id=1, source_target_pairs={{0,28},{4,0},{8,4},{12,8},{16,12},{20,16},{24,20},{28,24},{1,29},{... | collective-permute-start | bytes 3145736 | tf_op jit(solution)/shard_map/while/body/eval_jaxpr/ppermute | solution.py:10
  132.9 24.1 %collective-permute-start = (bf16[2,512,512]{2,1,0:T(8,128)(2,1)}, bf16[2,512,512]{2,1,0:T(8,128)(2,1)}, u32[]{:S(2)}, u32[]{:S(2)}) collective-permute-start(bf16[2,512,512]{2,1,0:T(8,128)(2,1)} %copy.26), channel_id=1, source_target_pairs={{0,3},{1,0},{2,1},{3,2},{4,7},{5,4},{6,5},{7,6},{8,11},{9,8},{10,9... | collective-permute-start | bytes 3145736 | tf_op jit(solution)/shard_map/while/body/eval_jaxpr/ppermute | solution.py:10
  136.8 20.2 %collective-permute-start.1 = (bf16[512,1024]{1,0:T(8,128)(2,1)S(1)}, bf16[512,1024]{1,0:T(8,128)(2,1)}, u32[]{:S(2)}, u32[]{:S(2)}) collective-permute-start(bf16[512,1024]{1,0:T(8,128)(2,1)S(1)} %copy.27), channel_id=1, source_target_pairs={{0,28},{4,0},{8,4},{12,8},{16,12},{20,16},{24,20},{28,24},{1,29},{... | collective-permute-start | bytes 3145736 | tf_op jit(solution)/shard_map/while/body/eval_jaxpr/ppermute | solution.py:10
  159.3 23.2 %collective-permute-start = (bf16[2,512,512]{2,1,0:T(8,128)(2,1)}, bf16[2,512,512]{2,1,0:T(8,128)(2,1)}, u32[]{:S(2)}, u32[]{:S(2)}) collective-permute-start(bf16[2,512,512]{2,1,0:T(8,128)(2,1)} %copy.26), channel_id=1, source_target_pairs={{0,3},{1,0},{2,1},{3,2},{4,7},{5,4},{6,5},{7,6},{8,11},{9,8},{10,9... | collective-permute-start | bytes 3145736 | tf_op jit(solution)/shard_map/while/body/eval_jaxpr/ppermute | solution.py:10
  163.2 19.3 %collective-permute-start.1 = (bf16[512,1024]{1,0:T(8,128)(2,1)S(1)}, bf16[512,1024]{1,0:T(8,128)(2,1)}, u32[]{:S(2)}, u32[]{:S(2)}) collective-permute-start(bf16[512,1024]{1,0:T(8,128)(2,1)S(1)} %copy.27), channel_id=1, source_target_pairs={{0,28},{4,0},{8,4},{12,8},{16,12},{20,16},{24,20},{28,24},{1,29},{... | collective-permute-start | bytes 3145736 | tf_op jit(solution)/shard_map/while/body/eval_jaxpr/ppermute | solution.py:10
  184.7 22.3 %collective-permute-start = (bf16[2,512,512]{2,1,0:T(8,128)(2,1)}, bf16[2,512,512]{2,1,0:T(8,128)(2,1)}, u32[]{:S(2)}, u32[]{:S(2)}) collective-permute-start(bf16[2,512,512]{2,1,0:T(8,128)(2,1)} %copy.26), channel_id=1, source_target_pairs={{0,3},{1,0},{2,1},{3,2},{4,7},{5,4},{6,5},{7,6},{8,11},{9,8},{10,9... | collective-permute-start | bytes 3145736 | tf_op jit(solution)/shard_map/while/body/eval_jaxpr/ppermute | solution.py:10
  188.6 18.4 %collective-permute-start.1 = (bf16[512,1024]{1,0:T(8,128)(2,1)S(1)}, bf16[512,1024]{1,0:T(8,128)(2,1)}, u32[]{:S(2)}, u32[]{:S(2)}) collective-permute-start(bf16[512,1024]{1,0:T(8,128)(2,1)S(1)} %copy.27), channel_id=1, source_target_pairs={{0,28},{4,0},{8,4},{12,8},{16,12},{20,16},{24,20},{28,24},{1,29},{... | collective-permute-start | bytes 3145736 | tf_op jit(solution)/shard_map/while/body/eval_jaxpr/ppermute | solution.py:10
  209.3 21.3 %collective-permute-start = (bf16[2,512,512]{2,1,0:T(8,128)(2,1)}, bf16[2,512,512]{2,1,0:T(8,128)(2,1)}, u32[]{:S(2)}, u32[]{:S(2)}) collective-permute-start(bf16[2,512,512]{2,1,0:T(8,128)(2,1)} %copy.26), channel_id=1, source_target_pairs={{0,3},{1,0},{2,1},{3,2},{4,7},{5,4},{6,5},{7,6},{8,11},{9,8},{10,9... | collective-permute-start | bytes 3145736 | tf_op jit(solution)/shard_map/while/body/eval_jaxpr/ppermute | solution.py:10
  213.1 17.5 %collective-permute-start.1 = (bf16[512,1024]{1,0:T(8,128)(2,1)S(1)}, bf16[512,1024]{1,0:T(8,128)(2,1)}, u32[]{:S(2)}, u32[]{:S(2)}) collective-permute-start(bf16[512,1024]{1,0:T(8,128)(2,1)S(1)} %copy.27), channel_id=1, source_target_pairs={{0,28},{4,0},{8,4},{12,8},{16,12},{20,16},{24,20},{28,24},{1,29},{... | collective-permute-start | bytes 3145736 | tf_op jit(solution)/shard_map/while/body/eval_jaxpr/ppermute | solution.py:10
  232.9 21.7 %collective-permute-start = (bf16[2,512,512]{2,1,0:T(8,128)(2,1)}, bf16[2,512,512]{2,1,0:T(8,128)(2,1)}, u32[]{:S(2)}, u32[]{:S(2)}) collective-permute-start(bf16[2,512,512]{2,1,0:T(8,128)(2,1)} %copy.26), channel_id=1, source_target_pairs={{0,3},{1,0},{2,1},{3,2},{4,7},{5,4},{6,5},{7,6},{8,11},{9,8},{10,9... | collective-permute-start | bytes 3145736 | tf_op jit(solution)/shard_map/while/body/eval_jaxpr/ppermute | solution.py:10
  236.7 17.8 %collective-permute-start.1 = (bf16[512,1024]{1,0:T(8,128)(2,1)S(1)}, bf16[512,1024]{1,0:T(8,128)(2,1)}, u32[]{:S(2)}, u32[]{:S(2)}) collective-permute-start(bf16[512,1024]{1,0:T(8,128)(2,1)S(1)} %copy.27), channel_id=1, source_target_pairs={{0,28},{4,0},{8,4},{12,8},{16,12},{20,16},{24,20},{28,24},{1,29},{... | collective-permute-start | bytes 3145736 | tf_op jit(solution)/shard_map/while/body/eval_jaxpr/ppermute | solution.py:10
where the time goes:
time: 260 us; the launch traced here: 258 us
  waiting for transfers between devices  144 us (55%)
  local copies, waits for them, and re-layouts  40.5 us (16%)
  blocking collectives  29.1 us (11%)
  starting transfers between devices  26.2 us (10%)
  matrix products  18 us (7%)
    ppermute x14, waiting for transfers between devices, passed_along(): return lax.ppermute(value, axis, pairs)  122 us
    while x14, local copies, waits for them, and re-layouts  24.4 us
    all_to_all x1, blocking collectives, shards(): lax.all_to_all(a_send, 'col', split_axis=0, concat_axis=0, tiled=True)  18.8 us
    all_to_all x1, waiting for transfers between devices, shards(): lax.all_to_all(b_send, 'row', split_axis=0, concat_axis=0, tiled=True)  18.4 us
    ppermute x14, starting transfers between devices, passed_along(): return lax.ppermute(value, axis, pairs)  16.8 us
    dot_general x7, matrix products, advance(): jnp.dot(a_use, panel_b, preferred_element_type=jnp.float32)  14.4 us
    all_to_all x1, blocking collectives, shards(): lax.all_to_all(b_tags, 'row', split_axis=0, concat_axis=0, tiled=True)  10.3 us
  transfers between devices with their start and end apart: 16, of which 9 were waited for; matrix products, arithmetic and copies ran while one was open for 12% of the time, Pallas kernels for 0%

commit v1 on v0

--- a/solution.py
+++ b/solution.py
@@ -51,8 +51,26 @@
     )
     b_send = b_blocks.reshape(row_count, -1, block_size, block_size)
     b_tags = b_coord.reshape(row_count, -1, 2)
+
+    def update_patches_on_mesh(unit):
+        step_out = lax.axis_size("row")
+        now = lax.axis_index("row")
+        y1, view_out = (step_out, now)
+        k_now = unit.shape[0] // y1
+        long_array = jnp.roll(unit, shift=-view_out * k_now, axis=0)
+        reached = lax.slice_in_dim(long_array, 0, k_now, axis=0)
+        sheets = [reached]
+        t = 1
+        while t < y1:
+            x_new = lax.slice_in_dim(long_array, t * k_now, (t + 1) * k_now, axis=0)
+            top = lax.ppermute(x_new, "row", [(u, (u + t) % y1) for u in range(y1)])
+            sheets.append(top)
+            t += 1
+        carry_in = jnp.concatenate(sheets[::-1], axis=0)
+        return jnp.roll(carry_in, shift=(view_out + 1) * sheets[0].shape[0], axis=0)
+
     b_recv, b_tags = (
-        lax.all_to_all(b_send, "row", split_axis=0, concat_axis=0, tiled=True),
+        update_patches_on_mesh(b_send),
         lax.all_to_all(b_tags, "row", split_axis=0, concat_axis=0, tiled=True),
     )
     b_recv = b_recv.reshape(-1, block_size, block_size)

time: 260 us -> 244 us (0.938)
  blocking collectives: 29.1 us -> 0 us
  starting transfers between devices: 26.2 us -> 38.9 us
  waiting for transfers between devices: 144 us -> 134 us
  local copies, waits for them, and re-layouts: 40.5 us -> 45 us
  other arithmetic: 0.05 us -> 4.13 us
    all_to_all x2 -> x0, blocking collectives: 29.1 us -> none  [the longest x1 18.8 us: shards(): lax.all_to_all(a_send, 'col', split_axis=0, concat_axis=0, tiled=True)]
    all_to_all x1 -> x2, waiting for transfers between devices: 18.4 us -> 4.92 us  [the longest x1 4.91 us: shards(): lax.all_to_all(b_tags, 'row', split_axis=0, concat_axis=0, tiled=True)]
    ppermute x0 -> x7, starting transfers between devices: none -> 8.88 us  [update_patches_on_mesh(): top = lax.ppermute(x_new, 'row', [(u, (u + t) % y1) for u in range(y1)])]
    ppermute x0 -> x7, waiting for transfers between devices: none -> 7.56 us  [update_patches_on_mesh(): top = lax.ppermute(x_new, 'row', [(u, (u + t) % y1) for u in range(y1)])]
    unnamed x3 -> x16, local copies, waits for them, and re-layouts: 1.29 us -> 5.04 us
    all_to_all x1 -> x2, starting transfers between devices: 4.24 us -> 7.55 us  [the longest x1 4.24 us: shards(): lax.all_to_all(a_send, 'col', split_axis=0, concat_axis=0, tiled=True)]
    concatenate x0 -> x2, other arithmetic: none -> 2.99 us  [the longest x1 1.63 us: update_patches_on_mesh(): long_array = jnp.roll(unit, shift=-view_out * k_now, axis=0)]
    ppermute x14, waiting for transfers between devices: 122 us -> 119 us  [passed_along(): return lax.ppermute(value, axis, pairs)]
  transfers between devices with their start and end apart: 16 -> 24, of which waited for: 9 -> 10; matrix products, arithmetic and copies ran while one was open for 12% -> 16% of each run, Pallas kernels for 0% -> 0%
where the time goes in v1:
time: 244 us; the launch traced here: 241 us
  waiting for transfers between devices  134 us (55%)
  local copies, waits for them, and re-layouts  45 us (18%)
  starting transfers between devices  38.9 us (16%)
  matrix products  18.1 us (7%)
  other arithmetic  4.13 us (2%)
    ppermute x14, waiting for transfers between devices, passed_along(): return lax.ppermute(value, axis, pairs)  119 us
    while x14, local copies, waits for them, and re-layouts  24.4 us
    ppermute x14, starting transfers between devices, passed_along(): return lax.ppermute(value, axis, pairs)  18.7 us
    dot_general x7, matrix products, advance(): jnp.dot(a_use, panel_b, preferred_element_type=jnp.float32)  14.5 us
    ppermute x7, starting transfers between devices, update_patches_on_mesh(): top = lax.ppermute(x_new, 'row', [(u, (u + t) % y1) for u in range(y1)])  8.88 us
    ppermute x7, waiting for transfers between devices, update_patches_on_mesh(): top = lax.ppermute(x_new, 'row', [(u, (u + t) % y1) for u in range(y1)])  7.56 us
    unnamed x16, local copies, waits for them, and re-layouts  5.04 us
    all_to_all x1, waiting for transfers between devices, shards(): lax.all_to_all(b_tags, 'row', split_axis=0, concat_axis=0, tiled=True)  4.91 us
  transfers between devices with their start and end apart: 24, of which 10 were waited for; matrix products, arithmetic and copies ran while one was open for 16% of the time, Pallas kernels for 0%

profile of v1, /device:TPU:0, one launch (start us, length us, event | category | flops | bytes accessed | tf_op | source)
XLA Modules:
  0.0 240.6 jit_solution(12129100189412566593)
XLA Ops:
  2.5 4.5 %collective-permute-start.2 = (bf16[1,4,128,128]{3,2,1,0:T(8,128)(2,1)}, bf16[1,4,128,128]{3,2,1,0:T(8,128)(2,1)}, u32[]{:S(2)}, u32[]{:S(2)}) collective-permute-start(bf16[1,4,128,128]{3,2,1,0:T(8,128)(2,1)} %get-tuple-element.180), channel_id=1, source_target_pairs={{0,28},{4,0},{8,4},{12,8},{16,12},{20,16},{24,20},{28,24},{1,29},{... | collective-permute-start | bytes 393224 | tf_op jit(solution)/shard_map/ppermute | solution.py:66
  7.5 2.8 %collective-permute-start.5 = (bf16[1,4,128,128]{3,2,1,0:T(8,128)(2,1)}, bf16[1,4,128,128]{3,2,1,0:T(8,128)(2,1)}, u32[]{:S(2)}, u32[]{:S(2)}) collective-permute-start(bf16[1,4,128,128]{3,2,1,0:T(8,128)(2,1)} %get-tuple-element.177), channel_id=1, source_target_pairs={{0,16},{4,20},{8,24},{12,28},{16,0},{20,4},{24,8},{28,12},{1,17},{... | collective-permute-start | bytes 393224 | tf_op jit(solution)/shard_map/ppermute | solution.py:66
  10.9 3.7 %all-to-all-start = ((s32[4,8,2]{1,2,0:T(2,128)}), s32[4,8,2]{1,2,0:T(2,128)S(1)}, u32[]{:S(2)}, u32[]{:S(2)}) async-start(s32[4,8,2]{1,2,0:T(2,128)} %copy.8), calls=%async_computation | async-start | bytes 8192 | tf_op jit(solution)/shard_map/all_to_all | solution.py:30
  16.6 2.7 %all-to-all-done = s32[4,8,2]{1,2,0:T(2,128)S(1)} async-done(((s32[4,8,2]{1,2,0:T(2,128)}), s32[4,8,2]{1,2,0:T(2,128)S(1)}, u32[]{:S(2)}, u32[]{:S(2)}) %all-to-all-start) | async-done | bytes 288 | tf_op jit(solution)/shard_map/all_to_all | solution.py:30
  19.3 3.3 %all-to-all-start.2 = ((s32[8,4,2]{1,2,0:T(2,128)}), s32[8,4,2]{1,2,0:T(2,128)S(1)}, u32[]{:S(2)}, u32[]{:S(2)}) async-start(s32[8,4,2]{1,2,0:T(2,128)} %copy.11), calls=%async_computation.2 | async-start | bytes 16384 | tf_op jit(solution)/shard_map/all_to_all | solution.py:74
  23.3 4.9 %all-to-all-done.2 = s32[8,4,2]{1,2,0:T(2,128)S(1)} async-done(((s32[8,4,2]{1,2,0:T(2,128)}), s32[8,4,2]{1,2,0:T(2,128)S(1)}, u32[]{:S(2)}, u32[]{:S(2)}) %all-to-all-start.2) | async-done | bytes 288 | tf_op jit(solution)/shard_map/all_to_all | solution.py:74
  28.2 4.2 %all-to-all-start.1 = ((bf16[4,8,128,128]{3,2,1,0:T(8,128)(2,1)}), bf16[4,8,128,128]{3,2,1,0:T(8,128)(2,1)}, u32[]{:S(2)}, u32[]{:S(2)}) async-start(bf16[4,8,128,128]{3,2,1,0:T(8,128)(2,1)} %bitcast.49), calls=%async_computation.1 | async-start | bytes 2097152 | tf_op jit(solution)/shard_map/all_to_all | solution.py:29
  37.4 7.5 %collective-permute-done.6 = bf16[1,4,128,128]{3,2,1,0:T(8,128)(2,1)S(1)} collective-permute-done((bf16[1,4,128,128]{3,2,1,0:T(8,128)(2,1)S(1)}, bf16[1,4,128,128]{3,2,1,0:T(8,128)(2,1)S(1)}, u32[]{:S(2)}, u32[]{:S(2)}) %collective-permute-start.6) | collective-permute-done | bytes 131104 | tf_op jit(solution)/shard_map/ppermute | solution.py:66
  46.6 3.6 %scatter_fusion.1 = bf16[32,128,128]{2,1,0:T(8,128)(2,1)S(1)} fusion(bf16[32,128,128]{2,1,0:T(8,128)(2,1)S(1)} %broadcast.70.clone.1, s32[32]{0:T(128)S(1)} %fusion.13, bf16[32,128,128]{2,1,0:T(8,128)(2,1)} %bitcast.46), kind=kCustom, calls=%fused_computation.1 | custom fusion | bytes 3145856 | tf_op jit(solution)/shard_map/scatter | solution.py:85
  52.4 3.6 %scatter_fusion = bf16[32,128,128]{2,1,0:T(8,128)(2,1)S(1)} fusion(bf16[32,128,128]{2,1,0:T(8,128)(2,1)S(1)} %broadcast.70.clone, s32[32]{0:T(128)S(1)} %copy-done.2, bf16[32,128,128]{2,1,0:T(8,128)(2,1)} %bitcast.2), kind=kCustom, calls=%fused_computation | custom fusion | bytes 3145856 | tf_op jit(solution)/shard_map/scatter | solution.py:46
  60.1 176.7 %while.20 = (s32[]{:T(128)}, bf16[2,512,512]{2,1,0:T(8,128)(2,1)}, bf16[512,1024]{1,0:T(8,128)(2,1)}, f32[512,1024]{1,0:T(8,128)S(1)}, s32[]{:T(128)}, /*index=5...) while((s32[]{:T(128)}, bf16[2,512,512]{2,1,0:T(8,128)(2,1)}, ...), condition=%wide.region_3.5_spmd.clone, body=%wide.region_2.4_spmd.clone.sunk | while | flops 537919488 | bytes 18350596 | solution.py:100
  62.3 2.9 %collective-permute-start = (bf16[2,512,512]{2,1,0:T(8,128)(2,1)}, bf16[2,512,512]{2,1,0:T(8,128)(2,1)}, u32[]{:S(2)}, u32[]{:S(2)}) collective-permute-start(bf16[2,512,512]{2,1,0:T(8,128)(2,1)} %copy.33), channel_id=1, source_target_pairs={{0,3},{1,0},{2,1},{3,2},{4,7},{5,4},{6,5},{7,6},{8,11},{9,8},{10,9... | collective-permute-start | bytes 3145736 | tf_op jit(solution)/shard_map/while/body/eval_jaxpr/ppermute | solution.py:10
  68.5 16.4 %collective-permute-done = bf16[2,512,512]{2,1,0:T(8,128)(2,1)} collective-permute-done((bf16[2,512,512]{2,1,0:T(8,128)(2,1)}, bf16[2,512,512]{2,1,0:T(8,128)(2,1)}, u32[]{:S(2)}, u32[]{:S(2)}) %collective-permute-start) | collective-permute-done | bytes 1048608 | tf_op jit(solution)/shard_map/while/body/eval_jaxpr/ppermute | solution.py:10
  87.2 3.4 %collective-permute-start = (bf16[2,512,512]{2,1,0:T(8,128)(2,1)}, bf16[2,512,512]{2,1,0:T(8,128)(2,1)}, u32[]{:S(2)}, u32[]{:S(2)}) collective-permute-start(bf16[2,512,512]{2,1,0:T(8,128)(2,1)} %copy.33), channel_id=1, source_target_pairs={{0,3},{1,0},{2,1},{3,2},{4,7},{5,4},{6,5},{7,6},{8,11},{9,8},{10,9... | collective-permute-start | bytes 3145736 | tf_op jit(solution)/shard_map/while/body/eval_jaxpr/ppermute | solution.py:10
  93.9 15.5 %collective-permute-done = bf16[2,512,512]{2,1,0:T(8,128)(2,1)} collective-permute-done((bf16[2,512,512]{2,1,0:T(8,128)(2,1)}, bf16[2,512,512]{2,1,0:T(8,128)(2,1)}, u32[]{:S(2)}, u32[]{:S(2)}) %collective-permute-start) | collective-permute-done | bytes 1048608 | tf_op jit(solution)/shard_map/while/body/eval_jaxpr/ppermute | solution.py:10
  111.7 3.4 %collective-permute-start = (bf16[2,512,512]{2,1,0:T(8,128)(2,1)}, bf16[2,512,512]{2,1,0:T(8,128)(2,1)}, u32[]{:S(2)}, u32[]{:S(2)}) collective-permute-start(bf16[2,512,512]{2,1,0:T(8,128)(2,1)} %copy.33), channel_id=1, source_target_pairs={{0,3},{1,0},{2,1},{3,2},{4,7},{5,4},{6,5},{7,6},{8,11},{9,8},{10,9... | collective-permute-start | bytes 3145736 | tf_op jit(solution)/shard_map/while/body/eval_jaxpr/ppermute | solution.py:10
  118.8 14.6 %collective-permute-done = bf16[2,512,512]{2,1,0:T(8,128)(2,1)} collective-permute-done((bf16[2,512,512]{2,1,0:T(8,128)(2,1)}, bf16[2,512,512]{2,1,0:T(8,128)(2,1)}, u32[]{:S(2)}, u32[]{:S(2)}) %collective-permute-start) | collective-permute-done | bytes 1048608 | tf_op jit(solution)/shard_map/while/body/eval_jaxpr/ppermute | solution.py:10
  133.4 2.3 copy.33
  135.7 2.9 %collective-permute-start = (bf16[2,512,512]{2,1,0:T(8,128)(2,1)}, bf16[2,512,512]{2,1,0:T(8,128)(2,1)}, u32[]{:S(2)}, u32[]{:S(2)}) collective-permute-start(bf16[2,512,512]{2,1,0:T(8,128)(2,1)} %copy.33), channel_id=1, source_target_pairs={{0,3},{1,0},{2,1},{3,2},{4,7},{5,4},{6,5},{7,6},{8,11},{9,8},{10,9... | collective-permute-start | bytes 3145736 | tf_op jit(solution)/shard_map/while/body/eval_jaxpr/ppermute | solution.py:10
  143.7 16.9 %collective-permute-done = bf16[2,512,512]{2,1,0:T(8,128)(2,1)} collective-permute-done((bf16[2,512,512]{2,1,0:T(8,128)(2,1)}, bf16[2,512,512]{2,1,0:T(8,128)(2,1)}, u32[]{:S(2)}, u32[]{:S(2)}) %collective-permute-start) | collective-permute-done | bytes 1048608 | tf_op jit(solution)/shard_map/while/body/eval_jaxpr/ppermute | solution.py:10
  167.7 19.2 %collective-permute-done = bf16[2,512,512]{2,1,0:T(8,128)(2,1)} collective-permute-done((bf16[2,512,512]{2,1,0:T(8,128)(2,1)}, bf16[2,512,512]{2,1,0:T(8,128)(2,1)}, u32[]{:S(2)}, u32[]{:S(2)}) %collective-permute-start) | collective-permute-done | bytes 1048608 | tf_op jit(solution)/shard_map/while/body/eval_jaxpr/ppermute | solution.py:10
  193.7 18.6 %collective-permute-done = bf16[2,512,512]{2,1,0:T(8,128)(2,1)} collective-permute-done((bf16[2,512,512]{2,1,0:T(8,128)(2,1)}, bf16[2,512,512]{2,1,0:T(8,128)(2,1)}, u32[]{:S(2)}, u32[]{:S(2)}) %collective-permute-start) | collective-permute-done | bytes 1048608 | tf_op jit(solution)/shard_map/while/body/eval_jaxpr/ppermute | solution.py:10
  219.1 17.7 %collective-permute-done = bf16[2,512,512]{2,1,0:T(8,128)(2,1)} collective-permute-done((bf16[2,512,512]{2,1,0:T(8,128)(2,1)}, bf16[2,512,512]{2,1,0:T(8,128)(2,1)}, u32[]{:S(2)}, u32[]{:S(2)}) %collective-permute-start) | collective-permute-done | bytes 1048608 | tf_op jit(solution)/shard_map/while/body/eval_jaxpr/ppermute | solution.py:10
  237.0 3.6 %bitcast_multiply_fusion = f32[512,1024]{1,0:T(8,128)} fusion(f32[64,8,8,128]{3,2,1,0:T(8,128)S(1)} %bitcast.45, f32[512,1024]{1,0:T(8,128)S(1)} %get-tuple-element.143, bf16[512,1024]{1,0:T(8,128)(2,1)} %get-tuple-element.145, bf16[2,512,512]{2,1,0:T(8,128)(2,1)} %get-tuple-element.144, s32[]{:T(128)S(6)} %select_n.110), kind=kOutput, calls=%fused_computation.6 | convolution fusion | flops 537919488 | bytes 7864324 | tf_op jit(solution)/shard_map/dot_general | solution.py:105
  (87 shorter events, 62.1 us)
Async XLA Ops:
  2.5 30.2 %collective-permute-start.2 = (bf16[1,4,128,128]{3,2,1,0:T(8,128)(2,1)}, bf16[1,4,128,128]{3,2,1,0:T(8,128)(2,1)}, u32[]{:S(2)}, u32[]{:S(2)}) collective-permute-start(bf16[1,4,128,128]{3,2,1,0:T(8,128)(2,1)} %get-tuple-element.180), channel_id=1, source_target_pairs={{0,28},{4,0},{8,4},{12,8},{16,12},{20,16},{24,20},{28,24},{1,29},{... | collective-permute-start | bytes 393224 | tf_op jit(solution)/shard_map/ppermute | solution.py:66
  7.0 27.2 %collective-permute-start.3 = (bf16[1,4,128,128]{3,2,1,0:T(8,128)(2,1)}, bf16[1,4,128,128]{3,2,1,0:T(8,128)(2,1)}, u32[]{:S(2)}, u32[]{:S(2)}) collective-permute-start(bf16[1,4,128,128]{3,2,1,0:T(8,128)(2,1)} %get-tuple-element.179), channel_id=1, source_target_pairs={{0,24},{4,28},{8,0},{12,4},{16,8},{20,12},{24,16},{28,20},{1,25},{... | collective-permute-start | bytes 393224 | tf_op jit(solution)/shard_map/ppermute | solution.py:66
  7.5 28.0 %collective-permute-start.4 = (bf16[1,4,128,128]{3,2,1,0:T(8,128)(2,1)}, bf16[1,4,128,128]{3,2,1,0:T(8,128)(2,1)}, u32[]{:S(2)}, u32[]{:S(2)}) collective-permute-start(bf16[1,4,128,128]{3,2,1,0:T(8,128)(2,1)} %get-tuple-element.178), channel_id=1, source_target_pairs={{0,20},{4,24},{8,28},{12,0},{16,4},{20,8},{24,12},{28,16},{1,21},{... | collective-permute-start | bytes 393224 | tf_op jit(solution)/shard_map/ppermute | solution.py:66
  7.5 28.9 %collective-permute-start.5 = (bf16[1,4,128,128]{3,2,1,0:T(8,128)(2,1)}, bf16[1,4,128,128]{3,2,1,0:T(8,128)(2,1)}, u32[]{:S(2)}, u32[]{:S(2)}) collective-permute-start(bf16[1,4,128,128]{3,2,1,0:T(8,128)(2,1)} %get-tuple-element.177), channel_id=1, source_target_pairs={{0,16},{4,20},{8,24},{12,28},{16,0},{20,4},{24,8},{28,12},{1,17},{... | collective-permute-start | bytes 393224 | tf_op jit(solution)/shard_map/ppermute | solution.py:66
  10.9 8.4 %all-to-all-start = ((s32[4,8,2]{1,2,0:T(2,128)}), s32[4,8,2]{1,2,0:T(2,128)S(1)}, u32[]{:S(2)}, u32[]{:S(2)}) async-start(s32[4,8,2]{1,2,0:T(2,128)} %copy.8), calls=%async_computation | async-start | bytes 8192 | tf_op jit(solution)/shard_map/all_to_all | solution.py:30
  19.3 8.9 %all-to-all-start.2 = ((s32[8,4,2]{1,2,0:T(2,128)}), s32[8,4,2]{1,2,0:T(2,128)S(1)}, u32[]{:S(2)}, u32[]{:S(2)}) async-start(s32[8,4,2]{1,2,0:T(2,128)} %copy.11), calls=%async_computation.2 | async-start | bytes 16384 | tf_op jit(solution)/shard_map/all_to_all | solution.py:74
  28.2 24.0 %all-to-all-start.1 = ((bf16[4,8,128,128]{3,2,1,0:T(8,128)(2,1)}), bf16[4,8,128,128]{3,2,1,0:T(8,128)(2,1)}, u32[]{:S(2)}, u32[]{:S(2)}) async-start(bf16[4,8,128,128]{3,2,1,0:T(8,128)(2,1)} %bitcast.49), calls=%async_computation.1 | async-start | bytes 2097152 | tf_op jit(solution)/shard_map/all_to_all | solution.py:29
  32.5 12.4 %collective-permute-start.6 = (bf16[1,4,128,128]{3,2,1,0:T(8,128)(2,1)S(1)}, bf16[1,4,128,128]{3,2,1,0:T(8,128)(2,1)S(1)}, u32[]{:S(2)}, u32[]{:S(2)}) collective-permute-start(bf16[1,4,128,128]{3,2,1,0:T(8,128)(2,1)S(1)} %get-tuple-element.176), channel_id=1, source_target_pairs={{0,12},{4,16},{8,20},{12,24},{16,28},{20,0},{24,4},{28,8},{1,13},{... | collective-permute-start | bytes 393224 | tf_op jit(solution)/shard_map/ppermute | solution.py:66
  33.5 11.4 %collective-permute-start.7 = (bf16[1,4,128,128]{3,2,1,0:T(8,128)(2,1)S(1)}, bf16[1,4,128,128]{3,2,1,0:T(8,128)(2,1)S(1)}, u32[]{:S(2)}, u32[]{:S(2)}) collective-permute-start(bf16[1,4,128,128]{3,2,1,0:T(8,128)(2,1)S(1)} %get-tuple-element.175), channel_id=1, source_target_pairs={{0,8},{4,12},{8,16},{12,20},{16,24},{20,28},{24,0},{28,4},{1,9},{5... | collective-permute-start | bytes 393224 | tf_op jit(solution)/shard_map/ppermute | solution.py:66
  35.1 9.9 %collective-permute-start.8 = (bf16[1,4,128,128]{3,2,1,0:T(8,128)(2,1)S(1)}, bf16[1,4,128,128]{3,2,1,0:T(8,128)(2,1)S(1)}, u32[]{:S(2)}, u32[]{:S(2)}) collective-permute-start(bf16[1,4,128,128]{3,2,1,0:T(8,128)(2,1)S(1)} %get-tuple-element.174), channel_id=1, source_target_pairs={{0,4},{4,8},{8,12},{12,16},{16,20},{20,24},{24,28},{28,0},{1,5},{5... | collective-permute-start | bytes 393224 | tf_op jit(solution)/shard_map/ppermute | solution.py:66
  62.3 22.6 %collective-permute-start = (bf16[2,512,512]{2,1,0:T(8,128)(2,1)}, bf16[2,512,512]{2,1,0:T(8,128)(2,1)}, u32[]{:S(2)}, u32[]{:S(2)}) collective-permute-start(bf16[2,512,512]{2,1,0:T(8,128)(2,1)} %copy.33), channel_id=1, source_target_pairs={{0,3},{1,0},{2,1},{3,2},{4,7},{5,4},{6,5},{7,6},{8,11},{9,8},{10,9... | collective-permute-start | bytes 3145736 | tf_op jit(solution)/shard_map/while/body/eval_jaxpr/ppermute | solution.py:10
  66.5 18.5 %collective-permute-start.1 = (bf16[512,1024]{1,0:T(8,128)(2,1)S(1)}, bf16[512,1024]{1,0:T(8,128)(2,1)}, u32[]{:S(2)}, u32[]{:S(2)}) collective-permute-start(bf16[512,1024]{1,0:T(8,128)(2,1)S(1)} %copy.34), channel_id=1, source_target_pairs={{0,28},{4,0},{8,4},{12,8},{16,12},{20,16},{24,20},{28,24},{1,29},{... | collective-permute-start | bytes 3145736 | tf_op jit(solution)/shard_map/while/body/eval_jaxpr/ppermute | solution.py:10
  87.2 22.2 %collective-permute-start = (bf16[2,512,512]{2,1,0:T(8,128)(2,1)}, bf16[2,512,512]{2,1,0:T(8,128)(2,1)}, u32[]{:S(2)}, u32[]{:S(2)}) collective-permute-start(bf16[2,512,512]{2,1,0:T(8,128)(2,1)} %copy.33), channel_id=1, source_target_pairs={{0,3},{1,0},{2,1},{3,2},{4,7},{5,4},{6,5},{7,6},{8,11},{9,8},{10,9... | collective-permute-start | bytes 3145736 | tf_op jit(solution)/shard_map/while/body/eval_jaxpr/ppermute | solution.py:10
  91.8 17.6 %collective-permute-start.1 = (bf16[512,1024]{1,0:T(8,128)(2,1)S(1)}, bf16[512,1024]{1,0:T(8,128)(2,1)}, u32[]{:S(2)}, u32[]{:S(2)}) collective-permute-start(bf16[512,1024]{1,0:T(8,128)(2,1)S(1)} %copy.34), channel_id=1, source_target_pairs={{0,28},{4,0},{8,4},{12,8},{16,12},{20,16},{24,20},{28,24},{1,29},{... | collective-permute-start | bytes 3145736 | tf_op jit(solution)/shard_map/while/body/eval_jaxpr/ppermute | solution.py:10
  111.7 21.7 %collective-permute-start = (bf16[2,512,512]{2,1,0:T(8,128)(2,1)}, bf16[2,512,512]{2,1,0:T(8,128)(2,1)}, u32[]{:S(2)}, u32[]{:S(2)}) collective-permute-start(bf16[2,512,512]{2,1,0:T(8,128)(2,1)} %copy.33), channel_id=1, source_target_pairs={{0,3},{1,0},{2,1},{3,2},{4,7},{5,4},{6,5},{7,6},{8,11},{9,8},{10,9... | collective-permute-start | bytes 3145736 | tf_op jit(solution)/shard_map/while/body/eval_jaxpr/ppermute | solution.py:10
  116.3 17.1 %collective-permute-start.1 = (bf16[512,1024]{1,0:T(8,128)(2,1)S(1)}, bf16[512,1024]{1,0:T(8,128)(2,1)}, u32[]{:S(2)}, u32[]{:S(2)}) collective-permute-start(bf16[512,1024]{1,0:T(8,128)(2,1)S(1)} %copy.34), channel_id=1, source_target_pairs={{0,28},{4,0},{8,4},{12,8},{16,12},{20,16},{24,20},{28,24},{1,29},{... | collective-permute-start | bytes 3145736 | tf_op jit(solution)/shard_map/while/body/eval_jaxpr/ppermute | solution.py:10
  135.7 25.0 %collective-permute-start = (bf16[2,512,512]{2,1,0:T(8,128)(2,1)}, bf16[2,512,512]{2,1,0:T(8,128)(2,1)}, u32[]{:S(2)}, u32[]{:S(2)}) collective-permute-start(bf16[2,512,512]{2,1,0:T(8,128)(2,1)} %copy.33), channel_id=1, source_target_pairs={{0,3},{1,0},{2,1},{3,2},{4,7},{5,4},{6,5},{7,6},{8,11},{9,8},{10,9... | collective-permute-start | bytes 3145736 | tf_op jit(solution)/shard_map/while/body/eval_jaxpr/ppermute | solution.py:10
  139.8 20.8 %collective-permute-start.1 = (bf16[512,1024]{1,0:T(8,128)(2,1)S(1)}, bf16[512,1024]{1,0:T(8,128)(2,1)}, u32[]{:S(2)}, u32[]{:S(2)}) collective-permute-start(bf16[512,1024]{1,0:T(8,128)(2,1)S(1)} %copy.34), channel_id=1, source_target_pairs={{0,28},{4,0},{8,4},{12,8},{16,12},{20,16},{24,20},{28,24},{1,29},{... | collective-permute-start | bytes 3145736 | tf_op jit(solution)/shard_map/while/body/eval_jaxpr/ppermute | solution.py:10
  162.9 24.0 %collective-permute-start = (bf16[2,512,512]{2,1,0:T(8,128)(2,1)}, bf16[2,512,512]{2,1,0:T(8,128)(2,1)}, u32[]{:S(2)}, u32[]{:S(2)}) collective-permute-start(bf16[2,512,512]{2,1,0:T(8,128)(2,1)} %copy.33), channel_id=1, source_target_pairs={{0,3},{1,0},{2,1},{3,2},{4,7},{5,4},{6,5},{7,6},{8,11},{9,8},{10,9... | collective-permute-start | bytes 3145736 | tf_op jit(solution)/shard_map/while/body/eval_jaxpr/ppermute | solution.py:10
  165.3 21.6 %collective-permute-start.1 = (bf16[512,1024]{1,0:T(8,128)(2,1)S(1)}, bf16[512,1024]{1,0:T(8,128)(2,1)}, u32[]{:S(2)}, u32[]{:S(2)}) collective-permute-start(bf16[512,1024]{1,0:T(8,128)(2,1)S(1)} %copy.34), channel_id=1, source_target_pairs={{0,28},{4,0},{8,4},{12,8},{16,12},{20,16},{24,20},{28,24},{1,29},{... | collective-permute-start | bytes 3145736 | tf_op jit(solution)/shard_map/while/body/eval_jaxpr/ppermute | solution.py:10
  189.2 23.1 %collective-permute-start = (bf16[2,512,512]{2,1,0:T(8,128)(2,1)}, bf16[2,512,512]{2,1,0:T(8,128)(2,1)}, u32[]{:S(2)}, u32[]{:S(2)}) collective-permute-start(bf16[2,512,512]{2,1,0:T(8,128)(2,1)} %copy.33), channel_id=1, source_target_pairs={{0,3},{1,0},{2,1},{3,2},{4,7},{5,4},{6,5},{7,6},{8,11},{9,8},{10,9... | collective-permute-start | bytes 3145736 | tf_op jit(solution)/shard_map/while/body/eval_jaxpr/ppermute | solution.py:10
  191.6 20.7 %collective-permute-start.1 = (bf16[512,1024]{1,0:T(8,128)(2,1)S(1)}, bf16[512,1024]{1,0:T(8,128)(2,1)}, u32[]{:S(2)}, u32[]{:S(2)}) collective-permute-start(bf16[512,1024]{1,0:T(8,128)(2,1)S(1)} %copy.34), channel_id=1, source_target_pairs={{0,28},{4,0},{8,4},{12,8},{16,12},{20,16},{24,20},{28,24},{1,29},{... | collective-permute-start | bytes 3145736 | tf_op jit(solution)/shard_map/while/body/eval_jaxpr/ppermute | solution.py:10
  214.6 22.2 %collective-permute-start = (bf16[2,512,512]{2,1,0:T(8,128)(2,1)}, bf16[2,512,512]{2,1,0:T(8,128)(2,1)}, u32[]{:S(2)}, u32[]{:S(2)}) collective-permute-start(bf16[2,512,512]{2,1,0:T(8,128)(2,1)} %copy.33), channel_id=1, source_target_pairs={{0,3},{1,0},{2,1},{3,2},{4,7},{5,4},{6,5},{7,6},{8,11},{9,8},{10,9... | collective-permute-start | bytes 3145736 | tf_op jit(solution)/shard_map/while/body/eval_jaxpr/ppermute | solution.py:10
  217.0 19.8 %collective-permute-start.1 = (bf16[512,1024]{1,0:T(8,128)(2,1)S(1)}, bf16[512,1024]{1,0:T(8,128)(2,1)}, u32[]{:S(2)}, u32[]{:S(2)}) collective-permute-start(bf16[512,1024]{1,0:T(8,128)(2,1)S(1)} %copy.34), channel_id=1, source_target_pairs={{0,28},{4,0},{8,4},{12,8},{16,12},{20,16},{24,20},{28,24},{1,29},{... | collective-permute-start | bytes 3145736 | tf_op jit(solution)/shard_map/while/body/eval_jaxpr/ppermute | solution.py:10
  (4 other events, 204.5 us)
